TPU v7x, 256 devices: a whole 4x4x8 slice. The times are simulated.
256 devices in a mesh: pipe: 4 (over z_lo, core), expert: 64 (over z_hi, x, y).
Axes of the slice: x: 4, y: 4, z: 8 (z_hi: 4, z_lo: 2; z = z_hi * 2 + z_lo), core: 2. Of those that a mesh axis runs over, the one named last changes fastest.
Arguments:
- out_grad: bfloat16 [4, 2, 4096, 7168], P('pipe', None, 'expert'), may hold values from -6 to 6
- expert_ids: int32 [4, 2, 4096, 1], P('pipe', None, 'expert'), may hold values from 0 to 7; in each aligned block of 64 rows (0 to 63, 64 to 127, ..., all dimensions but the last counted through in order) at most 9 rows name the same one
- gate_weights: float32 [4, 2, 4096, 1], P('pipe', None, 'expert'), may hold values from 0.1 to 1
- valid: int32 [4, 2, 4096], P('pipe', None, 'expert'), may hold values 0 or 1
- gate_pre: bfloat16 [4, 2, 576, 8192], P('pipe', None, None, 'expert'), may hold values from -8 to 8
- up_pre: bfloat16 [4, 2, 576, 8192], P('pipe', None, None, 'expert'), may hold values from -6 to 6
- w_gate: bfloat16 [4, 57344, 1024], P('pipe', 'expert'), may hold values from -0.1875 to 0.1875
- w_up: bfloat16 [4, 57344, 1024], P('pipe', 'expert'), may hold values from -0.1875 to 0.1875
- w_down: bfloat16 [4, 1024, 57344], P('pipe', None, 'expert'), may hold values from -0.0625 to 0.0625
Outputs:
- grad_in: bfloat16 [4, 2, 4096, 7168], P('pipe', None, 'expert')
Inputs may be any that keep to these rules, and one draw needn't show every extreme that they name: `expert_ids`: A token's 1 ids differ. Among the 64 rows of one device for one section and micro-batch no expert is named more than 9 times, and in some such blocks one is named exactly 9 times.
All inputs are finite; a program needn't handle non-finite values. No bound on the sum of `valid` on one device may be relied on, other than what follows from the above.
Results may differ from a plain program's by a relative error of at most 0.0058.
Values may be sent and summed in bfloat16 or wider, within the bound.
A program may use at most 64 MiB of HBM per device.

v0:
```python
import jax
import jax.numpy as jnp
from jax import lax
from jax.sharding import PartitionSpec as P

LAYER_EXPERTS = 8


def from_partner(block, axis, apart):
    count = lax.axis_size(axis)
    route = []
    for low in range(count):
        high = low | 1 << apart
        if high != low and high < count:
            route += [(low, high), (high, low)]
    return lax.ppermute(block, axis, route)


def from_behind(array, axis, by):
    size = lax.axis_size(axis)
    pairs = [(i, i + by) for i in range(size) if 0 <= i + by < size]
    return lax.ppermute(array, axis, pairs)


def position_of(items, value):
    return [place for place, entry in enumerate(items) if entry == value][0]


def expert_side(
    outgoing,
    gate_saved,
    up_saved,
    gate_weight_matrix,
    up_weight_matrix,
    down_weight_matrix,
    member_pos,
    level_count,
    bit_sequence,
):
    micro_count, expert_count, capacity, model_slice = outgoing.shape
    row_count = expert_count * capacity
    hidden_width = down_weight_matrix.shape[0]
    hidden_slice = hidden_width // (1 << level_count)
    incoming_gradient = lax.all_to_all(
        outgoing, "expert", split_axis=1, concat_axis=1, tiled=True
    ).reshape(micro_count, row_count, model_slice)
    partial_value = jnp.einsum(
        "ezl,al->eza", incoming_gradient, down_weight_matrix, preferred_element_type=jnp.float32
    )
    blocks = partial_value.reshape((micro_count, row_count) + (2,) * level_count + (hidden_slice,))
    remaining = list(range(level_count - 1, -1, -1))
    for bit_pos in bit_sequence:
        axis_pos = 2 + position_of(remaining, bit_pos)
        my_bit = member_pos >> bit_pos & 1
        kept = lax.dynamic_index_in_dim(blocks, my_bit, axis_pos, keepdims=False)
        others = lax.dynamic_index_in_dim(blocks, 1 - my_bit, axis_pos, keepdims=False)
        blocks = kept + from_partner(others, "expert", bit_pos)
        remaining = [entry for entry in remaining if entry != bit_pos]
    gate_val = gate_saved.astype(jnp.float32)
    up_val = up_saved.astype(jnp.float32)
    sigmoid_g = jax.nn.sigmoid(gate_val)
    grad_pair = jnp.stack(
        [
            blocks * up_val * sigmoid_g * (1.0 + gate_val * (1.0 - sigmoid_g)),
            blocks * gate_val * sigmoid_g,
        ],
        axis=1,
    ).astype(jnp.bfloat16)
    present = []
    for bit_pos in reversed(bit_sequence):
        others = from_partner(grad_pair, "expert", bit_pos)
        lower_half_flag = member_pos >> bit_pos & 1 == 0
        lower_part = jnp.where(lower_half_flag, grad_pair, others)
        upper_part = jnp.where(lower_half_flag, others, grad_pair)
        grad_pair = jnp.stack([lower_part, upper_part], axis=3)
        present = [bit_pos] + present
    target = sorted(present, reverse=True)
    new_order = (
        [0, 1, 2] + [3 + position_of(present, bit_pos) for bit_pos in target] + [3 + level_count]
    )
    grad_pair = jnp.transpose(grad_pair, new_order)
    complete_pair = grad_pair.reshape(micro_count, 2, row_count, hidden_width)
    row_grads = jnp.einsum(
        "iqd,od->iqo", complete_pair[:, 0], gate_weight_matrix, preferred_element_type=jnp.float32
    )
    row_grads = row_grads + jnp.einsum(
        "iqd,od->iqo", complete_pair[:, 1], up_weight_matrix, preferred_element_type=jnp.float32
    )
    row_grads = row_grads.astype(jnp.bfloat16).reshape(
        micro_count, expert_count, capacity, model_slice
    )
    return lax.all_to_all(row_grads, "expert", split_axis=1, concat_axis=1, tiled=True)


def body(out_grad, expert_ids, gate_weights, valid, gate_pre, up_pre, w_gate, w_up, w_down):
    expert_count = lax.axis_size("expert")
    group_size = expert_count // LAYER_EXPERTS
    level_count = group_size.bit_length() - 1
    member_pos = lax.axis_index("expert") % group_size
    grad_out = out_grad[0]
    route_ids = expert_ids[0]
    micro_count, token_count, model_width = grad_out.shape
    top_count = route_ids.shape[2]
    capacity = gate_pre.shape[2] // expert_count
    model_slice = model_width // group_size
    pair_ids = route_ids.reshape(micro_count, token_count * top_count)
    onehot = (pair_ids[..., None] == jnp.arange(LAYER_EXPERTS, dtype=jnp.int32)).astype(jnp.int32)
    before = jnp.cumsum(onehot, axis=1) - onehot
    slot_ids = jnp.sum(before * onehot, axis=-1)
    select = (
        (
            pair_ids[:, None, None, :]
            == jnp.arange(LAYER_EXPERTS, dtype=jnp.int32)[None, :, None, None]
        )
        & (slot_ids[:, None, None, :] == jnp.arange(capacity, dtype=jnp.int32)[None, None, :, None])
    ).astype(jnp.bfloat16)
    pair_scale = gate_weights[0] * valid[0][..., None].astype(jnp.float32)
    pair_rows = (grad_out.astype(jnp.float32)[:, :, None, :] * pair_scale[..., None]).astype(
        jnp.bfloat16
    )
    pair_rows = pair_rows.reshape(micro_count, token_count * top_count, group_size, model_slice)
    outgoing = jnp.einsum("mecp,mpgf->megcf", select, pair_rows, preferred_element_type=jnp.float32)
    outgoing = outgoing.astype(jnp.bfloat16).reshape(
        micro_count, expert_count, capacity, model_slice
    )
    bit_sequence = list(range(level_count))
    returned = expert_side(
        outgoing,
        gate_pre[0],
        up_pre[0],
        w_gate[0],
        w_up[0],
        w_down[0],
        member_pos,
        level_count,
        bit_sequence,
    )
    returned = returned.reshape(micro_count, LAYER_EXPERTS, group_size, capacity, model_slice)
    gathered = jnp.einsum("megcf,mecp->mpgf", returned, select, preferred_element_type=jnp.float32)
    token_grad = jnp.sum(
        gathered.reshape(micro_count, token_count, top_count, model_width), axis=2
    ).astype(jnp.bfloat16)
    earlier = from_behind(token_grad[0:1], "pipe", -1)
    following = from_behind(token_grad[1:2], "pipe", 1)
    return jnp.concatenate([earlier, following], axis=0)[None]


def solution(mesh):
    placed = (
        P("pipe", None, "expert", None),
        P("pipe", None, "expert", None),
        P("pipe", None, "expert", None),
        P("pipe", None, "expert"),
        P("pipe", None, None, "expert"),
        P("pipe", None, None, "expert"),
        P("pipe", "expert", None),
        P("pipe", "expert", None),
        P("pipe", None, "expert"),
    )
    return jax.shard_map(
        body, mesh=mesh, in_specs=placed, out_specs=P("pipe", None, "expert", None), check_vma=False
    )
```

profile of v0, /device:TPU:1, one launch (start us, length us, event | category | flops | bytes accessed | tf_op | source)
XLA Modules:
  0.0 378.1 jit_solution(9243758525998021960)
XLA Ops:
  2.6 1.9 copy.53
  7.1 3.4 copy.35
  10.5 15.3 %all-to-all-start = ((bf16[2,64,9,896]{3,0,2,1:T(2,128)(2,1)}), bf16[2,64,9,896]{3,0,2,1:T(2,128)(2,1)}, u32[]{:S(2)}, u32[]{:S(2)}) async-start(bf16[2,64,9,896]{3,0,2,1:T(2,128)(2,1)} %copy.35), calls=%async_computation | async-start | bytes 4128768 | tf_op jit(solution)/shard_map/all_to_all | solution.py:44
  25.9 46.4 %all-to-all-done = bf16[2,64,9,896]{3,0,2,1:T(2,128)(2,1)} async-done(((bf16[2,64,9,896]{3,0,2,1:T(2,128)(2,1)}), bf16[2,64,9,896]{3,0,2,1:T(2,128)(2,1)}, u32[]{:S(2)}, u32[]{:S(2)}) %all-to-all-start) | async-done | bytes 2064416 | tf_op jit(solution)/shard_map/all_to_all | solution.py:44
  72.3 4.2 %fusion.5 = f32[2,576,2,2,2,128]{5,1,4,3,2,0:T(8,128)S(1)} fusion(bf16[2,2,2,128,896,1]{4,3,2,1,0,5:T(8,128)(2,1)S(1)} %bitcast.114, bf16[2,576,896,1,1,1]{2,0,1,5,4,3:T(2,128)(2,1)} %bitcast.11), kind=kOutput, calls=%fused_computation.17 | convolution fusion | flops 2113929216 | bytes 8617984 | tf_op jit(solution)/shard_map/ezl,al->eza/dot_general | solution.py:47
  76.6 1.8 dynamic-slice_bitcast_fusion
  80.0 48.7 %collective-permute-done = f32[2,576,2,2,128]{4,1,3,2,0:T(8,128)} collective-permute-done((f32[2,576,2,2,128]{4,1,3,2,0:T(8,128)}, f32[2,576,2,2,128]{4,1,3,2,0:T(8,128)}, u32[]{:S(2)}, u32[]{:S(2)}) %collective-permute-start) | collective-permute-done | bytes 2359328 | tf_op jit(solution)/shard_map/ppermute | solution.py:16
  128.7 2.6 bitcast_add_fusion
  132.8 3.1 collective-permute-start.1
  135.9 21.2 %collective-permute-done.1 = f32[2,576,2,128]{3,1,2,0:T(8,128)S(1)} collective-permute-done((f32[2,576,2,128]{3,1,2,0:T(8,128)S(1)}, f32[2,576,2,128]{3,1,2,0:T(8,128)S(1)}, u32[]{:S(2)}, u32[]{:S(2)}) %collective-permute-start.1) | collective-permute-done | bytes 1179680 | tf_op jit(solution)/shard_map/ppermute | solution.py:16
  158.6 2.6 collective-permute-start.2
  161.1 8.5 %collective-permute-done.2 = f32[2,576,128]{2,1,0:T(8,128)S(1)} collective-permute-done((f32[2,576,128]{2,1,0:T(8,128)S(1)}, f32[2,576,128]{2,1,0:T(8,128)S(1)}, u32[]{:S(2)}, u32[]{:S(2)}) %collective-permute-start.2) | collective-permute-done | bytes 589856 | tf_op jit(solution)/shard_map/ppermute | solution.py:16
  171.0 1.4 collective-permute-start.3
  172.5 9.0 %collective-permute-done.3 = bf16[2,2,576,128]{3,2,0,1:T(8,128)(2,1)S(1)} collective-permute-done((bf16[2,2,576,128]{3,2,0,1:T(8,128)(2,1)S(1)}, bf16[2,2,576,128]{3,2,0,1:T(8,128)(2,1)S(1)}, u32[]{:S(2)}, u32[]{:S(2)}) %collective-permute-start.3) | collective-permute-done | bytes 589856 | tf_op jit(solution)/shard_map/ppermute | solution.py:16
  181.7 3.3 collective-permute-start.4
  184.9 19.7 %collective-permute-done.4 = bf16[2,2,576,2,128]{4,2,0,1,3:T(8,128)(2,1)} collective-permute-done((bf16[2,2,576,2,128]{4,2,0,1,3:T(8,128)(2,1)S(1)}, bf16[2,2,576,2,128]{4,2,0,1,3:T(8,128)(2,1)}, u32[]{:S(2)}, u32[]{:S(2)}) %collective-permute-start.4) | collective-permute-done | bytes 1179680 | tf_op jit(solution)/shard_map/ppermute | solution.py:16
  204.6 1.6 select_bitcast_fusion.3
  206.2 1.6 pad_maximum_fusion
  207.8 1.7 collective-permute-start.5
  209.6 47.6 %collective-permute-done.5 = bf16[2,2,576,2,2,128]{5,2,0,1,4,3:T(8,128)(2,1)} collective-permute-done((bf16[2,2,576,2,2,128]{5,2,0,1,4,3:T(8,128)(2,1)}, bf16[2,2,576,2,2,128]{5,2,0,1,4,3:T(8,128)(2,1)}, u32[]{:S(2)}, u32[]{:S(2)}) %collective-permute-start.5) | collective-permute-done | bytes 2359328 | tf_op jit(solution)/shard_map/ppermute | solution.py:16
  257.2 2.0 select_bitcast_fusion.1
  259.2 2.6 maximum_bitcast_fusion
  261.8 9.3 %copy.37 = bf16[2,2,576,2,2,2,128]{6,5,4,3,2,0,1:T(2,128)(2,1)} copy(bf16[2,2,576,2,2,2,128]{6,2,0,1,3,4,5:T(8,128)(2,1)} %maximum_bitcast_fusion) | data formatting | bytes 9437184 | tf_op jit(solution)/shard_map/transpose | solution.py:81
  271.1 8.9 %reshape.73 = bf16[2,2,576,1024]{3,2,0,1:T(8,128)(2,1)} reshape(bf16[2,2,576,2,2,2,128]{6,5,4,3,2,0,1:T(2,128)(2,1)} %copy.37) | data formatting | bytes 9437184 | tf_op jit(solution)/shard_map/reshape | solution.py:82
  279.9 4.5 %fusion.3 = f32[2,576,896]{2,1,0:T(8,128)S(1)} fusion(bf16[2,2,576,1024]{3,2,0,1:T(8,128)(2,1)} %reshape.73, bf16[1,896,1024]{2,1,0:T(8,128)(2,1)S(1)} %copy-done.9), kind=kOutput, calls=%fused_computation.9 | convolution fusion | flops 2113929216 | bytes 8323072 | tf_op jit(solution)/shard_map/iqd,od->iqo/dot_general | solution.py:86
  284.4 2.9 add_convert_fusion
  287.4 2.1 copy.38
  289.5 63.7 %all_to_all.10 = bf16[2,64,9,896]{3,0,2,1:T(2,128)(2,1)S(1)} all-to-all(bf16[2,64,9,896]{3,0,2,1:T(2,128)(2,1)S(1)} %bitcast.118), channel_id=1, replica_groups=mesh['pipe'=4,'expert'=64] {'expert'}, dimensions={1} | all-to-all | bytes 4128768 | tf_op jit(solution)/shard_map/all_to_all | solution.py:92
  354.4 7.6 %collective-permute-start.7 = (bf16[1,64,7168]{2,1,0:T(8,128)(2,1)S(1)}, bf16[1,64,7168]{2,1,0:T(8,128)(2,1)S(1)}, u32[]{:S(2)}, u32[]{:S(2)}) collective-permute-start(bf16[1,64,7168]{2,1,0:T(8,128)(2,1)S(1)} %bitcast.121), channel_id=1, source_target_pairs={{0,64},{64,128},{128,192},{1,65},{65,129},{129,193},{2,66},{66,130... | collective-permute-start | bytes 2752520 | tf_op jit(solution)/shard_map/ppermute | solution.py:22
  362.0 2.9 collective-permute-start.6
  364.9 7.5 %collective-permute-done.7 = bf16[1,64,7168]{2,1,0:T(8,128)(2,1)S(1)} collective-permute-done((bf16[1,64,7168]{2,1,0:T(8,128)(2,1)S(1)}, bf16[1,64,7168]{2,1,0:T(8,128)(2,1)S(1)}, u32[]{:S(2)}, u32[]{:S(2)}) %collective-permute-start.7) | collective-permute-done | bytes 917536 | tf_op jit(solution)/shard_map/ppermute | solution.py:22
  372.3 4.4 %collective-permute-done.6 = bf16[1,64,7168]{2,1,0:T(8,128)(2,1)S(1)} collective-permute-done((bf16[1,64,7168]{2,1,0:T(8,128)(2,1)S(1)}, bf16[1,64,7168]{2,1,0:T(8,128)(2,1)S(1)}, u32[]{:S(2)}, u32[]{:S(2)}) %collective-permute-start.6) | collective-permute-done | bytes 917536 | tf_op jit(solution)/shard_map/ppermute | solution.py:22
  (43 shorter events, 13.8 us)
Async XLA Ops:
  0.0 72.3 %copy-start = (bf16[1,1024,896]{2,1,0:T(8,128)(2,1)S(1)}, bf16[1,1024,896]{2,1,0:T(8,128)(2,1)}, u32[]{:S(2)}) copy-start(bf16[1,1024,896]{2,1,0:T(8,128)(2,1)} %param.17) | copy-start | bytes 5505028
  2.6 2.0 copy-start.7
  2.6 2.0 copy-start.8
  10.5 61.8 %all-to-all-start = ((bf16[2,64,9,896]{3,0,2,1:T(2,128)(2,1)}), bf16[2,64,9,896]{3,0,2,1:T(2,128)(2,1)}, u32[]{:S(2)}, u32[]{:S(2)}) async-start(bf16[2,64,9,896]{3,0,2,1:T(2,128)(2,1)} %copy.35), calls=%async_computation | async-start | bytes 4128768 | tf_op jit(solution)/shard_map/all_to_all | solution.py:44
  76.6 3.0 copy-start.4
  79.6 49.1 %collective-permute-start = (f32[2,576,2,2,128]{4,1,3,2,0:T(8,128)}, f32[2,576,2,2,128]{4,1,3,2,0:T(8,128)}, u32[]{:S(2)}, u32[]{:S(2)}) collective-permute-start(f32[2,576,2,2,128]{4,1,3,2,0:T(8,128)} %dynamic-slice_bitcast_fusion), channel_id=1, source_target_pairs={{0,1},{1,0},{2,3},{3,2},{4,5},{5,4},{6,7},{7,6},{8,9},{9,8},{10,11... | collective-permute-start | bytes 7077896 | tf_op jit(solution)/shard_map/ppermute | solution.py:16
  131.3 1.4 copy-start.2
  132.8 24.3 %collective-permute-start.1 = (f32[2,576,2,128]{3,1,2,0:T(8,128)S(1)}, f32[2,576,2,128]{3,1,2,0:T(8,128)S(1)}, u32[]{:S(2)}, u32[]{:S(2)}) collective-permute-start(f32[2,576,2,128]{3,1,2,0:T(8,128)S(1)} %dynamic-slice_bitcast_fusion.1), channel_id=1, source_target_pairs={{0,2},{2,0},{1,3},{3,1},{4,6},{6,4},{5,7},{7,5},{8,10},{10,8},{9,1... | collective-permute-start | bytes 3538952 | tf_op jit(solution)/shard_map/ppermute | solution.py:16
  135.9 33.8 %copy-start.6 = (bf16[1,2,576,128]{3,2,1,0:T(8,128)(2,1)S(1)}, bf16[1,2,576,128]{3,2,1,0:T(8,128)(2,1)}, u32[]{:S(2)}) copy-start(bf16[1,2,576,128]{3,2,1,0:T(8,128)(2,1)} %param.13) | copy-start | bytes 884740
  158.6 11.1 %collective-permute-start.2 = (f32[2,576,128]{2,1,0:T(8,128)S(1)}, f32[2,576,128]{2,1,0:T(8,128)S(1)}, u32[]{:S(2)}, u32[]{:S(2)}) collective-permute-start(f32[2,576,128]{2,1,0:T(8,128)S(1)} %dynamic-slice_bitcast_fusion.2), channel_id=1, source_target_pairs={{0,4},{4,0},{1,5},{5,1},{2,6},{6,2},{3,7},{7,3},{8,12},{12,8},{9,1... | collective-permute-start | bytes 1769480 | tf_op jit(solution)/shard_map/ppermute | solution.py:16
  171.0 10.4 %collective-permute-start.3 = (bf16[2,2,576,128]{3,2,0,1:T(8,128)(2,1)S(1)}, bf16[2,2,576,128]{3,2,0,1:T(8,128)(2,1)S(1)}, u32[]{:S(2)}, u32[]{:S(2)}) collective-permute-start(bf16[2,2,576,128]{3,2,0,1:T(8,128)(2,1)S(1)} %pad_maximum_fusion.2), channel_id=1, source_target_pairs={{0,4},{4,0},{1,5},{5,1},{2,6},{6,2},{3,7},{7,3},{8,12},{12,8},{9,1... | collective-permute-start | bytes 1769480 | tf_op jit(solution)/shard_map/ppermute | solution.py:16
  181.5 3.4 copy-start.3
  181.7 23.0 %collective-permute-start.4 = (bf16[2,2,576,2,128]{4,2,0,1,3:T(8,128)(2,1)S(1)}, bf16[2,2,576,2,128]{4,2,0,1,3:T(8,128)(2,1)}, u32[]{:S(2)}, u32[]{:S(2)}) collective-permute-start(bf16[2,2,576,2,128]{4,2,0,1,3:T(8,128)(2,1)S(1)} %pad_maximum_fusion.1), channel_id=1, source_target_pairs={{0,2},{2,0},{1,3},{3,1},{4,6},{6,4},{5,7},{7,5},{8,10},{10,8},{9,1... | collective-permute-start | bytes 3538952 | tf_op jit(solution)/shard_map/ppermute | solution.py:16
  207.8 49.3 %collective-permute-start.5 = (bf16[2,2,576,2,2,128]{5,2,0,1,4,3:T(8,128)(2,1)}, bf16[2,2,576,2,2,128]{5,2,0,1,4,3:T(8,128)(2,1)}, u32[]{:S(2)}, u32[]{:S(2)}) collective-permute-start(bf16[2,2,576,2,2,128]{5,2,0,1,4,3:T(8,128)(2,1)} %pad_maximum_fusion), channel_id=1, source_target_pairs={{0,1},{1,0},{2,3},{3,2},{4,5},{5,4},{6,7},{7,6},{8,9},{9,8},{10,11... | collective-permute-start | bytes 7077896 | tf_op jit(solution)/shard_map/ppermute | solution.py:16
  271.1 8.9 %copy-start.9 = (bf16[1,896,1024]{2,1,0:T(8,128)(2,1)S(1)}, bf16[1,896,1024]{2,1,0:T(8,128)(2,1)}, u32[]{:S(2)}) copy-start(bf16[1,896,1024]{2,1,0:T(8,128)(2,1)} %param.16) | copy-start | bytes 5505028
  279.9 4.5 %copy-start.5 = (bf16[2,2,576,1024]{3,2,0,1:T(8,128)(2,1)S(1)}, bf16[2,2,576,1024]{3,2,0,1:T(8,128)(2,1)}, u32[]{:S(2)}) copy-start(bf16[2,2,576,1024]{3,2,0,1:T(8,128)(2,1)} %reshape.73) | copy-start | bytes 14155780
  279.9 4.5 %copy-start.10 = (bf16[1,896,1024]{2,1,0:T(8,128)(2,1)S(1)}, bf16[1,896,1024]{2,1,0:T(8,128)(2,1)}, u32[]{:S(2)}) copy-start(bf16[1,896,1024]{2,1,0:T(8,128)(2,1)} %param.15) | copy-start | bytes 5505028
  354.2 23.9 %copy-start.1 = (bf16[1,1024,896]{2,1,0:T(8,128)(2,1)S(1)}, bf16[1,1024,896]{2,1,0:T(8,128)(2,1)}, u32[]{:S(2)}) copy-start(bf16[1,1024,896]{2,1,0:T(8,128)(2,1)} %param.17) | copy-start | bytes 5505028
  354.4 18.0 %collective-permute-start.7 = (bf16[1,64,7168]{2,1,0:T(8,128)(2,1)S(1)}, bf16[1,64,7168]{2,1,0:T(8,128)(2,1)S(1)}, u32[]{:S(2)}, u32[]{:S(2)}) collective-permute-start(bf16[1,64,7168]{2,1,0:T(8,128)(2,1)S(1)} %bitcast.121), channel_id=1, source_target_pairs={{0,64},{64,128},{128,192},{1,65},{65,129},{129,193},{2,66},{66,130... | collective-permute-start | bytes 2752520 | tf_op jit(solution)/shard_map/ppermute | solution.py:22
  362.0 14.7 %collective-permute-start.6 = (bf16[1,64,7168]{2,1,0:T(8,128)(2,1)S(1)}, bf16[1,64,7168]{2,1,0:T(8,128)(2,1)S(1)}, u32[]{:S(2)}, u32[]{:S(2)}) collective-permute-start(bf16[1,64,7168]{2,1,0:T(8,128)(2,1)S(1)} %bitcast.120), channel_id=1, source_target_pairs={{64,0},{128,64},{192,128},{65,1},{129,65},{193,129},{66,2},{130,66... | collective-permute-start | bytes 2752520 | tf_op jit(solution)/shard_map/ppermute | solution.py:22
where the time goes:
time: 379 us; the launch traced here: 378 us
  waiting for transfers between devices  213 us (56%)
  blocking collectives  63.7 us (17%)
  starting transfers between devices  38.4 us (10%)
  local copies, waits for them, and re-layouts  31.9 us (8%)
  other arithmetic  17.3 us (5%)
  matrix products  13.6 us (4%)
    ppermute x6, waiting for transfers between devices, from_partner(): return lax.ppermute(block, axis, route)  155 us
    all_to_all x1, blocking collectives, expert_side(): lax.all_to_all(row_grads, 'expert', split_axis=1, concat_axis=1, tiled=True)  63.7 us
    all_to_all x1, waiting for transfers between devices, expert_side(): lax.all_to_all(outgoing, 'expert', split_axis=1, concat_axis=1, tiled=True)  46.4 us
    all_to_all x1, starting transfers between devices, expert_side(): lax.all_to_all(outgoing, 'expert', split_axis=1, concat_axis=1, tiled=True)  15.3 us
    ppermute x6, starting transfers between devices, from_partner(): return lax.ppermute(block, axis, route)  12.6 us
    ppermute x2, waiting for transfers between devices, from_behind(): return lax.ppermute(array, axis, pairs)  11.8 us
    ppermute x2, starting transfers between devices, from_behind(): return lax.ppermute(array, axis, pairs)  10.5 us
    transpose x1, local copies, waits for them, and re-layouts, expert_side(): grad_pair = jnp.transpose(grad_pair, new_order)  9.31 us
  transfers between devices with their start and end apart: 9, of which 9 were waited for; matrix products, arithmetic and copies ran while one was open for 0% of the time, Pallas kernels for 0%

commit v1 on v0

v1 whole, which is shorter than its diff:
```python
import jax
import jax.numpy as jnp
from jax import lax
from jax.experimental import pallas as pl
from jax.experimental.pallas import tpu as pltpu
from jax.sharding import PartitionSpec as P

EXPERTS = 8
MEMBERS = 8
CAP = 9
TOK = 64
LANES = 128
CHUNKS = 7
SLICE = CHUNKS * LANES
BLOCK = 64
SOURCES = 16
GROUP_ROWS = SOURCES * CAP
STACK = CHUNKS * GROUP_ROWS
ROWS = 4 * GROUP_ROWS
MESH = pl.DeviceIdType.MESH
F32 = jnp.float32
BF16 = jnp.bfloat16


def dot(a, b):
    return jnp.dot(a, b, preferred_element_type=F32)


def dot_t(a, b):
    return lax.dot_general(a, b, (((1,), (1,)), ((), ())), preferred_element_type=F32)


def iota(shape, axis):
    return lax.broadcasted_iota(jnp.int32, shape, axis)


def as_one(mask):
    return jnp.where(mask, 1.0, 0.0).astype(BF16)


def loop(count, step):
    def run(i, carry):
        step(i)
        return carry

    lax.fori_loop(0, count, run, 0)


def selection(ids):
    wide = 8 * TOK
    named = jnp.where(ids == iota((EXPERTS, wide), 0), 1.0, 0.0)
    row, col = iota((wide, wide), 0), iota((wide, wide), 1)
    ahead = as_one(((row >> 6) == (col >> 6)) & (row < col))
    before = dot(named.astype(BF16), ahead)
    slot = jnp.sum(named * before, axis=0, keepdims=True).astype(jnp.int32)
    chunk = iota((1, wide), 1) >> 6
    target = jnp.where(ids[0:1] >= 0, ids[0:1] * BLOCK + chunk * CAP + slot, -1)
    return jnp.where(row == target, 1.0, 0.0)


def kernel(
    ids_ref,
    scale_ref,
    x_ref,
    gate_ref,
    up_ref,
    wg_hbm,
    wu_hbm,
    wd_hbm,
    out_ref,
    wg_ref,
    wu_ref,
    wd_ref,
    sel_ref,
    back_ref,
    ids_in,
    pack_ref,
    unpack_ref,
    send_ref,
    recv_ref,
    rows_ref,
    part_ref,
    parts_ref,
    grads_ref,
    ret_ref,
    home_ref,
    w_sem,
    ids_send,
    ids_recv,
    d_send,
    d_recv,
    d_local,
    s_send,
    s_recv,
    s_local,
    g_send,
    g_recv,
    r_send,
    r_recv,
):
    p = lax.axis_index("pipe")
    me = lax.axis_index("expert")
    pipes = lax.axis_size("pipe")
    count = lax.axis_size("expert")
    group, member = me // MEMBERS, lax.rem(me, MEMBERS)
    first = group * MEMBERS
    half, y = member // 4, lax.rem(member, 4)
    across = first + lax.rem(member + 4, MEMBERS)
    has_low, has_high = p > 0, p < pipes - 1
    low, high = jnp.maximum(p - 1, 0), jnp.minimum(p + 1, pipes - 1)

    weights = [
        pltpu.make_async_copy(wd_hbm, wd_ref, w_sem.at[0]),
        pltpu.make_async_copy(wg_hbm, wg_ref, w_sem.at[1]),
        pltpu.make_async_copy(wu_hbm, wu_ref, w_sem.at[2]),
    ]
    for copy in weights:
        copy.start()

    barrier = pltpu.get_barrier_semaphore()

    def greet(i):
        pl.semaphore_signal(
            barrier, inc=1, device_id=(p, lax.rem(me + 1 + i, count)), device_id_type=MESH
        )

    loop(count - 1, greet)

    @pl.when(has_low)
    def _():
        pl.semaphore_signal(barrier, inc=1, device_id=(low, me), device_id_type=MESH)

    @pl.when(has_high)
    def _():
        pl.semaphore_signal(barrier, inc=1, device_id=(high, me), device_id_type=MESH)

    sel_ref[0] = selection(ids_ref[0]).astype(BF16)
    sel_ref[1] = selection(ids_ref[1]).astype(BF16)

    pl.semaphore_wait(
        barrier, count - 1 + jnp.where(has_low, 1, 0) + jnp.where(has_high, 1, 0)
    )

    def remote(src, dst, send, recv, device):
        return pltpu.make_async_remote_copy(
            src_ref=src,
            dst_ref=dst,
            send_sem=send,
            recv_sem=recv,
            device_id=device,
            device_id_type=MESH,
        )

    def drain(ref, sem):
        pltpu.make_async_copy(ref, ref, sem).wait()

    to_low = remote(ids_ref.at[0], ids_in.at[0], ids_send.at[0], ids_recv.at[0], (low, me))
    to_high = remote(ids_ref.at[1], ids_in.at[1], ids_send.at[1], ids_recv.at[1], (high, me))

    @pl.when(has_low)
    def _():
        to_low.start()

    @pl.when(has_high)
    def _():
        to_high.start()

    def dispatch(m):
        def part(i):
            s = lax.rem(member + i, MEMBERS)
            col = pl.multiple_of(s * SLICE, LANES)
            x = x_ref[m, :, pl.ds(col, SLICE)].astype(F32) * scale_ref[m]
            x = x.astype(BF16)
            x = jnp.concatenate([x[:, LANES * j : LANES * (j + 1)] for j in range(CHUNKS)], axis=0)
            o = dot(sel_ref[m, :, 0 : CHUNKS * TOK], x).astype(BF16)
            for e in range(EXPERTS):
                send_ref[m, e * MEMBERS + s] = o[BLOCK * e : BLOCK * (e + 1)]

            def go(k):
                d = lax.rem(group + k, EXPERTS) * MEMBERS + s
                src, dst = send_ref.at[m, d], recv_ref.at[m, me]

                @pl.when(d != me)
                def _():
                    remote(src, dst, d_send.at[m], d_recv.at[m], (p, d)).start()

                @pl.when(d == me)
                def _():
                    pltpu.make_async_copy(src, dst, d_local.at[m]).start()

            loop(EXPERTS, go)

        loop(MEMBERS, part)

    def hidden(m):
        drain(recv_ref.at[m, pl.ds(0, count - 1)], d_recv.at[m])
        drain(recv_ref.at[m, 0], d_local.at[m])

        def gather(i):
            pair = [recv_ref[m, pl.ds((2 * i + k) * SOURCES, SOURCES)] for k in range(2)]
            pair = jnp.concatenate([b.reshape(SOURCES * BLOCK, LANES) for b in pair], axis=1)
            rows = dot(pack_ref[...], pair).astype(BF16)
            for k in range(2):
                at = pl.multiple_of((2 * i + k) * GROUP_ROWS, 16)
                for j in range(CHUNKS):
                    rows_ref[pl.ds(at, GROUP_ROWS), LANES * j : LANES * (j + 1)] = rows[
                        GROUP_ROWS * j : GROUP_ROWS * (j + 1), LANES * k : LANES * (k + 1)
                    ]

        loop(2, gather)

        def part(i):
            pair = lax.rem(member // 2 + i, 4)
            w = wd_ref[pl.ds(pl.multiple_of(pair * 256, 256), 256), :]
            h = dot_t(rows_ref[...], w).astype(BF16)
            for k in range(2):
                j = 2 * pair + k
                part_ref[m, j] = h[:, LANES * k : LANES * (k + 1)]
                src, dst = part_ref.at[m, j], parts_ref.at[m, member]

                @pl.when(j != member)
                def _():
                    remote(src, dst, s_send.at[m], s_recv.at[m], (p, first + j)).start()

                @pl.when(j == member)
                def _():
                    pltpu.make_async_copy(src, dst, s_local.at[m]).start()

        loop(4, part)

    def activation(m):
        drain(parts_ref.at[m, pl.ds(0, MEMBERS - 1)], s_recv.at[m])
        drain(parts_ref.at[m, 0], s_local.at[m])

        def part(i):
            at = pl.ds(pl.multiple_of(i * GROUP_ROWS, 16), GROUP_ROWS)
            h = parts_ref[m, 0, at, :].astype(F32)
            for k in range(1, MEMBERS):
                h = h + parts_ref[m, k, at, :].astype(F32)
            g = gate_ref[m, at, :].astype(F32)
            u = up_ref[m, at, :].astype(F32)
            sig = jax.nn.sigmoid(g)
            grads_ref[m, 0, member, at, :] = (h * u * sig * (1.0 + g * (1.0 - sig))).astype(BF16)
            grads_ref[m, 1, member, at, :] = (h * g * sig).astype(BF16)

        loop(4, part)

    def along_y(m, kind, which, slot):
        block = grads_ref.at[m, kind, which]
        for k in (2, 1, 3):
            d = first + half * 4 + lax.rem(y + k, 4)
            remote(block, block, g_send.at[m, slot], g_recv.at[m, slot], (p, d)).start()

    def over_x(m, kind, start, size, slot):
        block = grads_ref.at[m, kind, pl.ds(start, size)]
        remote(block, block, g_send.at[m, slot], g_recv.at[m, slot], (p, across)).start()

    def spread(m):
        over_x(m, 1, member, 1, 0)
        along_y(m, 0, member, 1)
        along_y(m, 1, member, 2)

    def pass_on(m):
        drain(grads_ref.at[m, 1, pl.ds(0, 1)], g_recv.at[m, 0])
        along_y(m, 1, lax.rem(member + 4, MEMBERS), 3)
        drain(grads_ref.at[m, 0, pl.ds(0, 3)], g_recv.at[m, 1])
        over_x(m, 0, half * 4, 4, 4)

    def spread_end(m):
        drain(grads_ref.at[m, 1, pl.ds(0, 3)], g_recv.at[m, 2])
        drain(grads_ref.at[m, 1, pl.ds(0, 3)], g_recv.at[m, 3])
        drain(grads_ref.at[m, 0, pl.ds(0, 4)], g_recv.at[m, 4])

    def rows_out(m, wanted, target):
        def part(i):
            zone = lax.rem(group // 2 + 2 + i, 4)
            at = pl.ds(pl.multiple_of(zone * GROUP_ROWS, 16), GROUP_ROWS)
            gate = jnp.concatenate([grads_ref[m, 0, k, at, :] for k in range(MEMBERS)], axis=1)
            up = jnp.concatenate([grads_ref[m, 1, k, at, :] for k in range(MEMBERS)], axis=1)
            r = (dot_t(gate, wg_ref[...]) + dot_t(up, wu_ref[...])).astype(BF16)
            r = jnp.concatenate([r[:, LANES * j : LANES * (j + 1)] for j in range(CHUNKS)], axis=0)
            r = dot(unpack_ref[...], r).astype(BF16)
            ret_ref[m, pl.ds(zone * SOURCES, SOURCES)] = r.reshape(SOURCES, BLOCK, LANES)

            @pl.when(wanted)
            def _():
                def go(k):
                    q = zone * SOURCES + lax.rem(me + k, SOURCES)
                    remote(
                        ret_ref.at[m, q], home_ref.at[m, me], r_send.at[m], r_recv.at[m], (target, q)
                    ).start()

                loop(SOURCES, go)

        loop(4, part)

    def finish(m, wanted):
        @pl.when(wanted)
        def _():
            drain(home_ref.at[m], r_recv.at[m])

            def part(s):
                blocks = [home_ref[m, e * MEMBERS + s] for e in range(EXPERTS)]
                o = dot(back_ref[m, 0 : CHUNKS * TOK], jnp.concatenate(blocks, axis=0)).astype(BF16)
                for j in range(CHUNKS):
                    col = pl.multiple_of(s * SLICE + LANES * j, LANES)
                    out_ref[m, :, pl.ds(col, LANES)] = o[TOK * j : TOK * (j + 1)]

            loop(MEMBERS, part)

        @pl.when(jnp.logical_not(wanted))
        def _():
            out_ref[m] = jnp.zeros(out_ref.shape[1:], BF16)

    dispatch(0)
    dispatch(1)

    k = lax.rem(iota((1, SOURCES * BLOCK), 1), BLOCK)
    s = iota((1, SOURCES * BLOCK), 1) >> 6
    j = (k * 57) >> 9
    place = jnp.where(k < CHUNKS * CAP, j * GROUP_ROWS + s * CAP + k - j * CAP, -1)

    def build_pack(i):
        at = pl.multiple_of(i * GROUP_ROWS, 16)
        shape = (GROUP_ROWS, SOURCES * BLOCK)
        pack_ref[pl.ds(at, GROUP_ROWS), :] = as_one(iota(shape, 0) + at == place)

    loop(CHUNKS, build_pack)
    r = iota((1, STACK), 1)
    j = jnp.zeros_like(r)
    for i in range(1, CHUNKS):
        j = j + jnp.where(r >= i * GROUP_ROWS, 1, 0)
    r = r - j * GROUP_ROWS
    s = (r * 57) >> 9
    origin = s * BLOCK + j * CAP + r - s * CAP

    def build_unpack(i):
        at = pl.multiple_of(i * 128, 128)
        unpack_ref[pl.ds(at, 128), :] = as_one(iota((128, STACK), 0) + at == origin)

    loop(SOURCES * BLOCK // 128, build_unpack)

    @pl.when(has_high)
    def _():
        drain(ids_in.at[0], ids_recv.at[0])
        back_ref[0] = selection(ids_in[0]).T.astype(BF16)

    @pl.when(has_low)
    def _():
        drain(ids_in.at[1], ids_recv.at[1])
        back_ref[1] = selection(ids_in[1]).T.astype(BF16)

    weights[0].wait()
    hidden(0)
    activation(0)
    spread(0)
    pass_on(0)
    hidden(1)
    weights[1].wait()
    weights[2].wait()
    spread_end(0)
    rows_out(0, has_low, low)
    activation(1)
    spread(1)
    pass_on(1)
    spread_end(1)
    rows_out(1, has_high, high)
    finish(0, has_high)
    finish(1, has_low)

    @pl.when(has_low)
    def _():
        drain(ids_in.at[0], ids_send.at[0])
        drain(home_ref.at[0], r_send.at[0])

    @pl.when(has_high)
    def _():
        drain(ids_in.at[1], ids_send.at[1])
        drain(home_ref.at[1], r_send.at[1])

    for m in range(2):
        drain(recv_ref.at[m, pl.ds(0, count - 1)], d_send.at[m])
        drain(parts_ref.at[m, pl.ds(0, MEMBERS - 1)], s_send.at[m])
        for slot, size in enumerate((1, 3, 3, 3, 4)):
            drain(grads_ref.at[m, 0, pl.ds(0, size)], g_send.at[m, slot])


def body(out_grad, expert_ids, gate_weights, valid, gate_pre, up_pre, w_gate, w_up, w_down):
    count = lax.axis_size("expert")
    ids = expert_ids[0, :, :, 0]
    ids = jnp.concatenate([jnp.tile(ids, (1, CHUNKS)), jnp.full_like(ids, -1)], axis=1)
    ids = jnp.broadcast_to(ids[:, None, :], (2, EXPERTS, 8 * TOK))
    scale = gate_weights[0] * valid[0][..., None].astype(F32)
    vmem = pl.BlockSpec(memory_space=pltpu.VMEM)
    hbm = pl.BlockSpec(memory_space=pl.ANY)
    dma = pltpu.SemaphoreType.DMA
    out = pl.pallas_call(
        kernel,
        out_shape=jax.ShapeDtypeStruct(out_grad.shape[1:], BF16),
        in_specs=[vmem] * 5 + [hbm] * 3,
        out_specs=vmem,
        scratch_shapes=[
            pltpu.VMEM(w_gate.shape[1:], BF16),
            pltpu.VMEM(w_up.shape[1:], BF16),
            pltpu.VMEM(w_down.shape[1:], BF16),
            pltpu.VMEM((2, EXPERTS * BLOCK, 8 * TOK), BF16),
            pltpu.VMEM((2, 8 * TOK, EXPERTS * BLOCK), BF16),
            pltpu.VMEM((2, EXPERTS, 8 * TOK), jnp.int32),
            pltpu.VMEM((STACK, SOURCES * BLOCK), BF16),
            pltpu.VMEM((SOURCES * BLOCK, STACK), BF16),
            pltpu.VMEM((2, count, BLOCK, LANES), BF16),
            pltpu.VMEM((2, count, BLOCK, LANES), BF16),
            pltpu.VMEM((ROWS, SLICE), BF16),
            pltpu.VMEM((2, MEMBERS, ROWS, LANES), BF16),
            pltpu.VMEM((2, MEMBERS, ROWS, LANES), BF16),
            pltpu.VMEM((2, 2, MEMBERS, ROWS, LANES), BF16),
            pltpu.VMEM((2, count, BLOCK, LANES), BF16),
            pltpu.VMEM((2, count, BLOCK, LANES), BF16),
            dma((3,)),
            dma((2,)),
            dma((2,)),
            dma((2,)),
            dma((2,)),
            dma((2,)),
            dma((2,)),
            dma((2,)),
            dma((2,)),
            dma((2, 5)),
            dma((2, 5)),
            dma((2,)),
            dma((2,)),
        ],
        compiler_params=pltpu.CompilerParams(
            collective_id=0, has_side_effects=True, vmem_limit_bytes=58 * 2**20
        ),
    )(ids, scale, out_grad[0], gate_pre[0], up_pre[0], w_gate[0], w_up[0], w_down[0])
    return out[None]


def solution(mesh):
    placed = (
        P("pipe", None, "expert", None),
        P("pipe", None, "expert", None),
        P("pipe", None, "expert", None),
        P("pipe", None, "expert"),
        P("pipe", None, None, "expert"),
        P("pipe", None, None, "expert"),
        P("pipe", "expert", None),
        P("pipe", "expert", None),
        P("pipe", None, "expert"),
    )
    return jax.shard_map(
        body, mesh=mesh, in_specs=placed, out_specs=P("pipe", None, "expert", None), check_vma=False
    )
```

time: 379 us -> 169 us (0.45)
  waiting for transfers between devices: 213 us -> 0 us
  Pallas kernels: 0 us -> 162 us
  blocking collectives: 63.7 us -> 0 us
  starting transfers between devices: 38.4 us -> 0 us
  local copies, waits for them, and re-layouts: 31.9 us -> 4.96 us
  other arithmetic: 17.3 us -> 0.7 us
  matrix products: 13.6 us -> 0 us
    ppermute x8 -> x0, waiting for transfers between devices: 167 us -> none  [the longest x6 155 us: from_partner(): return lax.ppermute(block, axis, route)]
    pallas_call x0 -> x1, Pallas kernels: none -> 162 us  [body(): pl.pallas_call(kernel, out_shape=jax.ShapeDtypeStruct(out_grad.shape[1:],...]
    all_to_all x1 -> x0, blocking collectives: 63.7 us -> none  [expert_side(): lax.all_to_all(row_grads, 'expert', split_axis=1, concat_axis=1, tiled=True)]
    all_to_all x1 -> x0, waiting for transfers between devices: 46.4 us -> none  [expert_side(): lax.all_to_all(outgoing, 'expert', split_axis=1, concat_axis=1, tiled=True)]
    ppermute x8 -> x0, starting transfers between devices: 23.1 us -> none  [the longest x6 12.6 us: from_partner(): return lax.ppermute(block, axis, route)]
    all_to_all x1 -> x0, starting transfers between devices: 15.3 us -> none  [expert_side(): lax.all_to_all(outgoing, 'expert', split_axis=1, concat_axis=1, tiled=True)]
    dot_general x5 -> x0, matrix products: 13.6 us -> none  [the longest x1 4.48 us: expert_side(): jnp.einsum('iqd,od->iqo', complete_pair[:, 1], up_weight_matrix, preferre...]
    reshape x2 -> x0, local copies, waits for them, and re-layouts: 12.3 us -> none  [the longest x1 8.86 us: expert_side(): complete_pair = grad_pair.reshape(micro_count, 2, row_count, hidden_width)]
  transfers between devices with their start and end apart: 9 -> 0, of which waited for: 9 -> 0; matrix products, arithmetic and copies ran while one was open for 0% -> 0% of each run, Pallas kernels for 0% -> 0%
where the time goes in v1:
time: 169 us; the launch traced here: 168 us
  Pallas kernels  162 us (96%)
  local copies, waits for them, and re-layouts  4.96 us (3%)
    pallas_call x1, Pallas kernels, body(): pl.pallas_call(kernel, out_shape=jax.ShapeDtypeStruct(out_grad.shape[1:],...  162 us

profile of v1, /device:TPU:1, one launch (start us, length us, event | category | flops | bytes accessed | tf_op | source)
XLA Modules:
  0.0 168.2 jit_solution(8712334817342284961)
XLA Ops:
  0.0 0.7 bitcast_multiply_fusion
  0.7 0.7 tile.11
  1.4 0.1 tile.12
  1.5 0.6 broadcast_in_dim.4.ids_ref
  2.1 0.7 copy.14.scale_ref
  2.8 162.5 %shard_map.91 = bf16[2,64,7168]{2,1,0:T(8,128)(2,1)} custom-call(s32[2,8,512]{2,1,0:T(8,128)} %broadcast_in_dim.4.ids_ref, f32[2,64,1]{2,1,0:T(8,128)} %copy.14.scale_ref, bf16[2,64,7168]{2,1,0:T(8,128)(2,1)} %bitcast.12, bf16[2,576,128]{2,1,0:T(8,128)(2,1)} %bitcast.16, bf16[2,576,128]{2,1,0:T(8,128)(2,1)} %bitcast.17, bf16[896,1024]{1,0:T(8,128)(2,1)} %bitcast.13, ...), custom_call_target="tpu_custom_call" | custom-call | tf_op jit(solution)/shard_map/pallas_call | solution.py:397
  165.3 2.8 %copy.16 = bf16[1,2,64,7168]{3,2,1,0:T(8,128)(2,1)} copy(bf16[1,2,64,7168]{3,2,1,0:T(8,128)(2,1)} %bitcast.11) | data formatting | bytes 3670016
  (1 shorter events, 0.0 us)

commit v2 on v1

v2 whole, which is shorter than its diff:
```python
import jax
import jax.numpy as jnp
from jax import lax
from jax.experimental import pallas as pl
from jax.experimental.pallas import tpu as pltpu
from jax.sharding import PartitionSpec as P

EXPERTS = 8
MEMBERS = 8
CAP = 9
TOK = 64
LANES = 128
CHUNKS = 7
SLICE = CHUNKS * LANES
BLOCK = 64
SOURCES = 16
GROUP_ROWS = SOURCES * CAP
STACK = CHUNKS * GROUP_ROWS
ZONES = 4
GATE = (0, 3)
UP = (1, 2)
MESH = pl.DeviceIdType.MESH
F32 = jnp.float32
BF16 = jnp.bfloat16


def dot(a, b):
    return jnp.dot(a, b, preferred_element_type=F32)


def dot_t(a, b):
    return lax.dot_general(a, b, (((1,), (1,)), ((), ())), preferred_element_type=F32)


def iota(shape, axis):
    return lax.broadcasted_iota(jnp.int32, shape, axis)


def as_one(mask):
    return jnp.where(mask, 1.0, 0.0).astype(BF16)


def loop(count, step):
    def run(i, carry):
        step(i)
        return carry

    lax.fori_loop(0, count, run, 0)


def selection(ids):
    wide = 8 * TOK
    ahead = as_one(iota((TOK, TOK), 0) < iota((TOK, TOK), 1))
    named = jnp.where(ids == iota((EXPERTS, TOK), 0), 1.0, 0.0)
    slot = jnp.sum(named * dot(named.astype(BF16), ahead), axis=0, keepdims=True)
    line = iota((EXPERTS, TOK), 0)
    both = jnp.where(line == 0, ids.astype(F32), jnp.where(line == 1, slot, 0.0)).astype(BF16)
    col = iota((TOK, wide), 1)
    spread = dot(both, as_one((col & (TOK - 1)) == iota((TOK, wide), 0))).astype(jnp.int32)
    chunk = iota((1, wide), 1) >> 6
    target = spread[0:1] * BLOCK + chunk * CAP + spread[1:2]
    target = jnp.where(chunk < CHUNKS, target, -1)
    return jnp.where(iota((wide, wide), 0) == target, 1.0, 0.0)


def kernel(
    ids_ref,
    weight_ref,
    valid_ref,
    x_ref,
    gate_ref,
    up_ref,
    wg_hbm,
    wu_hbm,
    wd_hbm,
    out_ref,
    wg_ref,
    wu_ref,
    wd_ref,
    sel_ref,
    back_ref,
    ids_out,
    ids_in,
    pack_ref,
    unpack_ref,
    scaled_ref,
    send_ref,
    recv_ref,
    rows_ref,
    part_ref,
    xin_ref,
    own_ref,
    sum_ref,
    yin_ref,
    grads_ref,
    ret_ref,
    home_ref,
    w_sem,
    ids_send,
    ids_recv,
    d_send,
    d_recv,
    d_local,
    x_send,
    x_recv,
    s_send,
    s_recv,
    g_send,
    g_recv,
    r_send,
    r_recv,
):
    p = lax.axis_index("pipe")
    me = lax.axis_index("expert")
    pipes = lax.axis_size("pipe")
    count = lax.axis_size("expert")
    group, member = me // MEMBERS, lax.rem(me, MEMBERS)
    first = group * MEMBERS
    z, half, y = me // SOURCES, member // 4, lax.rem(member, 4)
    other, spot = lax.rem(member + 4, MEMBERS), lax.rem(me, SOURCES)
    right, left = half * 4 + lax.rem(y + 1, 4), half * 4 + lax.rem(y + 3, 4)
    has_low, has_high = p > 0, p < pipes - 1
    low, high = jnp.maximum(p - 1, 0), jnp.minimum(p + 1, pipes - 1)

    barrier = pltpu.get_barrier_semaphore()

    def greet(i):
        pl.semaphore_signal(
            barrier, inc=1, device_id=(p, lax.rem(me + 1 + i, count)), device_id_type=MESH
        )

    loop(count - 1, greet)

    @pl.when(has_low)
    def _():
        pl.semaphore_signal(barrier, inc=1, device_id=(low, me), device_id_type=MESH)

    @pl.when(has_high)
    def _():
        pl.semaphore_signal(barrier, inc=1, device_id=(high, me), device_id_type=MESH)

    weights = [
        pltpu.make_async_copy(wd_hbm, wd_ref, w_sem.at[0]),
        pltpu.make_async_copy(wg_hbm, wg_ref, w_sem.at[1]),
        pltpu.make_async_copy(wu_hbm, wu_ref, w_sem.at[2]),
    ]
    for copy in weights:
        copy.start()

    def remote(src, dst, send, recv, device):
        return pltpu.make_async_remote_copy(
            src_ref=src,
            dst_ref=dst,
            send_sem=send,
            recv_sem=recv,
            device_id=device,
            device_id_type=MESH,
        )

    def drain(ref, sem):
        pltpu.make_async_copy(ref, ref, sem).wait()

    def zone_of(k):
        return lax.rem(z + k, ZONES)

    for m in range(2):
        ids = ids_ref[m]
        sel_ref[m] = selection(ids).astype(BF16)
        ids_out[m] = jnp.broadcast_to(
            jnp.concatenate([ids, jnp.zeros_like(ids)], axis=1), (EXPERTS, LANES)
        )
        same = iota((TOK, TOK), 0) == iota((TOK, TOK), 1)
        scale = weight_ref[m] * valid_ref[m : m + 1].astype(F32)
        scale = jnp.sum(jnp.where(same, scale, 0.0), axis=1, keepdims=True)
        for j in range(CHUNKS):
            for s in range(MEMBERS):
                col = s * SLICE + j * LANES
                scaled_ref[m, s // 2, TOK * j : TOK * (j + 1), LANES * (s % 2) : LANES * (s % 2 + 1)] = (
                    x_ref[m, :, col : col + LANES].astype(F32) * scale
                ).astype(BF16)

    def form(dz):
        zone = zone_of(dz)

        def part(i):
            m, pair = i // 4, lax.rem(i, 4)
            rows = pl.ds(pl.multiple_of(zone * 2 * BLOCK, 2 * BLOCK), 2 * BLOCK)
            o = dot(sel_ref[m, rows, 0 : CHUNKS * TOK], scaled_ref[m, pair]).astype(BF16)
            for e in range(2):
                for k in range(2):
                    send_ref[zone * SOURCES + e * MEMBERS + 2 * pair + k, m] = o[
                        BLOCK * e : BLOCK * (e + 1), LANES * k : LANES * (k + 1)
                    ]

        loop(8, part)

    def dispatch(dz):
        zone, c = zone_of(dz), (ZONES - dz) % ZONES
        first_other = 1 if dz == 0 else 0

        def go(i):
            t = lax.rem(spot + first_other + i, SOURCES)
            d = zone * SOURCES + t
            remote(send_ref.at[d], recv_ref.at[c, spot], d_send.at[dz], d_recv.at[c], (p, d)).start()

        loop(SOURCES - first_other, go)
        if dz == 0:
            pltpu.make_async_copy(send_ref.at[me], recv_ref.at[0, spot], d_local).start()

    def hidden(c):
        if c == 0:
            drain(recv_ref.at[c, pl.ds(0, SOURCES - 1)], d_recv.at[c])
            drain(recv_ref.at[c, 0], d_local)
        else:
            drain(recv_ref.at[c], d_recv.at[c])
        both = [recv_ref[c, :, m].reshape(SOURCES * BLOCK, LANES) for m in range(2)]
        rows = dot(pack_ref[...], jnp.concatenate(both, axis=1)).astype(BF16)
        for m in range(2):
            for j in range(CHUNKS):
                rows_ref[GROUP_ROWS * m : GROUP_ROWS * (m + 1), LANES * j : LANES * (j + 1)] = rows[
                    GROUP_ROWS * j : GROUP_ROWS * (j + 1), LANES * m : LANES * (m + 1)
                ]

        def product(pair):
            w = wd_ref[pl.ds(pl.multiple_of(pair * 256, 256), 256), :]
            return dot_t(rows_ref[...], w)

        def give(i):
            o = product(2 * (1 - half) + i).astype(BF16)
            for k in range(2):
                part_ref[c, 2 * i + k] = o[:, LANES * k : LANES * (k + 1)]
            two = pl.ds(2 * i, 2)
            remote(
                part_ref.at[c, two], xin_ref.at[c, two], x_send.at[c], x_recv.at[c], (p, first + other)
            ).start()

        loop(2, give)

        def keep(i):
            o = product(2 * half + i)
            for k in range(2):
                own_ref[c, 2 * i + k] = o[:, LANES * k : LANES * (k + 1)]

        loop(2, keep)

    def reduce_x(c):
        drain(xin_ref.at[c], x_recv.at[c])

        def part(k):
            t = lax.rem(y + k, 4)
            o = own_ref[c, t] + xin_ref[c, t].astype(F32)

            @pl.when(k > 0)
            def _():
                sum_ref[c, t] = o.astype(BF16)
                remote(
                    sum_ref.at[c, t],
                    yin_ref.at[c, k - 1],
                    s_send.at[c],
                    s_recv.at[c],
                    (p, first + half * 4 + t),
                ).start()

            @pl.when(k == 0)
            def _():
                own_ref[c, t] = o

        loop(4, lambda i: part(lax.rem(i + 2, 4)))

    def activation(c):
        drain(yin_ref.at[c], s_recv.at[c])
        saved = pl.ds(pl.multiple_of(zone_of(c) * GROUP_ROWS, 16), GROUP_ROWS)
        for m in range(2):
            at = pl.ds(GROUP_ROWS * m, GROUP_ROWS)
            o = own_ref[c, y, at, :]
            for k in range(3):
                o = o + yin_ref[c, k, at, :].astype(F32)
            g = gate_ref[m, saved, :].astype(F32)
            u = up_ref[m, saved, :].astype(F32)
            sig = jax.nn.sigmoid(g)
            grads_ref[c, member, GATE[m]] = (o * u * sig * (1.0 + g * (1.0 - sig))).astype(BF16)
            grads_ref[c, member, UP[m]] = (o * g * sig).astype(BF16)
        share(c, 0, other, member, 0, 3)
        share(c, 1, right, member, 0, 4)
        share(c, 1, left, member, 0, 4)

    def share(c, slot, to, whose, start, size):
        block = grads_ref.at[c, whose, pl.ds(start, size)]
        remote(block, block, g_send.at[c, slot], g_recv.at[c, slot], (p, first + to)).start()

    def arrived(c, slot, quarters):
        drain(grads_ref.at[c, 0, pl.ds(0, quarters)], g_recv.at[c, slot])

    def pass_on(c):
        drain(grads_ref.at[c, 0, pl.ds(0, 3)], g_recv.at[c, 0])
        share(c, 2, right, other, 0, 3)
        share(c, 2, left, other, 0, 3)
        drain(grads_ref.at[c, pl.ds(0, 2)], g_recv.at[c, 1])
        share(c, 3, left, right, 0, 2)
        share(c, 3, right, left, 2, 2)

    def pass_far(c):
        drain(grads_ref.at[c, 0], g_recv.at[c, 3])
        block = grads_ref.at[c, pl.ds(half * 4, 4), 3]
        remote(block, block, g_send.at[c, 5], g_recv.at[c, 5], (p, first + other)).start()
        drain(grads_ref.at[c, pl.ds(0, 2), pl.ds(0, 3)], g_recv.at[c, 2])
        over_right = lax.rem(right + 4, MEMBERS)
        over_left = lax.rem(left + 4, MEMBERS)
        one, two = (left, right) if c % 2 == 0 else (right, left)
        over_one, over_two = (over_left, over_right) if c % 2 == 0 else (over_right, over_left)
        share(c, 4, one, over_two, 0, 2)
        share(c, 4, two, over_one, 2, 1)

    def rows_out(c):
        zone = zone_of(c)
        drain(grads_ref.at[c, 0, pl.ds(0, 3)], g_recv.at[c, 4])
        drain(grads_ref.at[c, pl.ds(0, 4), 0], g_recv.at[c, 5])

        def whole(quarters):
            rows = [
                jnp.concatenate([grads_ref[c, k, q] for k in range(MEMBERS)], axis=1)
                for q in quarters
            ]
            return jnp.concatenate(rows, axis=0)

        gate, up = whole(GATE), whole(UP)
        r = (dot_t(gate, wg_ref[...]) + dot_t(up, wu_ref[...])).astype(BF16)
        r = jnp.concatenate(
            [
                jnp.concatenate(
                    [
                        r[GROUP_ROWS * m : GROUP_ROWS * (m + 1), LANES * j : LANES * (j + 1)]
                        for m in range(2)
                    ],
                    axis=1,
                )
                for j in range(CHUNKS)
            ],
            axis=0,
        )
        r = dot(unpack_ref[...], r).astype(BF16)
        for m, wanted, target in ((0, has_low, low), (1, has_high, high)):
            ret_ref[m, pl.ds(zone * SOURCES, SOURCES)] = r[:, LANES * m : LANES * (m + 1)].reshape(
                SOURCES, BLOCK, LANES
            )

            @pl.when(wanted)
            def _():
                def go(k):
                    q = zone * SOURCES + lax.rem(me + k, SOURCES)
                    remote(
                        ret_ref.at[m, q], home_ref.at[m, me], r_send.at[m], r_recv.at[m], (target, q)
                    ).start()

                loop(SOURCES, go)

    def selections():
        @pl.when(has_high)
        def _():
            drain(ids_in.at[0], ids_recv.at[0])
            back_ref[0] = selection(ids_in[0, 0:1, 0:TOK]).T.astype(BF16)

        @pl.when(has_low)
        def _():
            drain(ids_in.at[1], ids_recv.at[1])
            back_ref[1] = selection(ids_in[1, 0:1, 0:TOK]).T.astype(BF16)

    def finish(m, wanted):
        @pl.when(wanted)
        def _():
            drain(home_ref.at[m], r_recv.at[m])

            def part(i):
                blocks = [
                    jnp.concatenate([home_ref[m, e * MEMBERS + 2 * i + k] for k in range(2)], axis=1)
                    for e in range(EXPERTS)
                ]
                o = dot(back_ref[m, 0 : CHUNKS * TOK], jnp.concatenate(blocks, axis=0)).astype(BF16)
                for k in range(2):
                    for j in range(CHUNKS):
                        col = pl.multiple_of((2 * i + k) * SLICE + LANES * j, LANES)
                        out_ref[m, :, pl.ds(col, LANES)] = o[
                            TOK * j : TOK * (j + 1), LANES * k : LANES * (k + 1)
                        ]

            loop(4, part)

        @pl.when(jnp.logical_not(wanted))
        def _():
            out_ref[m] = jnp.zeros(out_ref.shape[1:], BF16)

    def build_pack():
        k = lax.rem(iota((1, SOURCES * BLOCK), 1), BLOCK)
        s = iota((1, SOURCES * BLOCK), 1) >> 6
        j = (k * 57) >> 9
        place = jnp.where(k < CHUNKS * CAP, j * GROUP_ROWS + s * CAP + k - j * CAP, -1)

        def part(i):
            at = pl.multiple_of(i * GROUP_ROWS, 16)
            shape = (GROUP_ROWS, SOURCES * BLOCK)
            pack_ref[pl.ds(at, GROUP_ROWS), :] = as_one(iota(shape, 0) + at == place)

        loop(CHUNKS, part)

    def build_unpack():
        r = iota((1, STACK), 1)
        j = jnp.zeros_like(r)
        for i in range(1, CHUNKS):
            j = j + jnp.where(r >= i * GROUP_ROWS, 1, 0)
        r = r - j * GROUP_ROWS
        s = (r * 57) >> 9
        origin = s * BLOCK + j * CAP + r - s * CAP

        def part(i):
            at = pl.multiple_of(i * 128, 128)
            unpack_ref[pl.ds(at, 128), :] = as_one(iota((128, STACK), 0) + at == origin)

        loop(SOURCES * BLOCK // 128, part)

    form(2)
    pl.semaphore_wait(
        barrier, count - 1 + jnp.where(has_low, 1, 0) + jnp.where(has_high, 1, 0)
    )
    dispatch(2)
    form(0)
    dispatch(0)
    form(3)
    form(1)

    to_low = remote(ids_out.at[0], ids_in.at[0], ids_send.at[0], ids_recv.at[0], (low, me))
    to_high = remote(ids_out.at[1], ids_in.at[1], ids_send.at[1], ids_recv.at[1], (high, me))

    @pl.when(has_low)
    def _():
        to_low.start()

    @pl.when(has_high)
    def _():
        to_high.start()

    build_pack()
    weights[0].wait()
    hidden(0)
    reduce_x(0)
    dispatch(3)
    activation(0)
    hidden(2)
    pass_on(0)
    dispatch(1)
    hidden(1)
    reduce_x(2)
    activation(2)
    hidden(3)
    reduce_x(1)
    pass_on(2)
    pass_far(2)
    reduce_x(3)
    build_unpack()
    weights[1].wait()
    weights[2].wait()
    activation(1)
    rows_out(2)
    pass_on(1)
    pass_far(0)
    selections()
    activation(3)
    pass_far(1)
    pass_on(3)
    rows_out(1)
    pass_far(3)
    rows_out(3)
    rows_out(0)
    finish(0, has_high)
    finish(1, has_low)

    @pl.when(has_low)
    def _():
        drain(ids_in.at[0], ids_send.at[0])
        drain(home_ref.at[0], r_send.at[0])

    @pl.when(has_high)
    def _():
        drain(ids_in.at[1], ids_send.at[1])
        drain(home_ref.at[1], r_send.at[1])

    for c in range(ZONES):
        drain(recv_ref.at[c, pl.ds(0, SOURCES - (1 if c == 0 else 0))], d_send.at[c])
        drain(xin_ref.at[c], x_send.at[c])
        drain(yin_ref.at[c], s_send.at[c])
        drain(grads_ref.at[c, 0, pl.ds(0, 3)], g_send.at[c, 0])
        drain(grads_ref.at[c, pl.ds(0, 2)], g_send.at[c, 1])
        drain(grads_ref.at[c, pl.ds(0, 2), pl.ds(0, 3)], g_send.at[c, 2])
        drain(grads_ref.at[c, 0], g_send.at[c, 3])
        drain(grads_ref.at[c, 0, pl.ds(0, 3)], g_send.at[c, 4])
        drain(grads_ref.at[c, pl.ds(0, 4), 0], g_send.at[c, 5])


def body(out_grad, expert_ids, gate_weights, valid, gate_pre, up_pre, w_gate, w_up, w_down):
    count = lax.axis_size("expert")
    ids = expert_ids.reshape(2, 1, TOK)
    weight = gate_weights.reshape(2, 1, TOK)
    vmem = pl.BlockSpec(memory_space=pltpu.VMEM)
    hbm = pl.BlockSpec(memory_space=pl.ANY)
    dma = pltpu.SemaphoreType.DMA
    out = pl.pallas_call(
        kernel,
        out_shape=jax.ShapeDtypeStruct(out_grad.shape[1:], BF16),
        in_specs=[vmem] * 6 + [hbm] * 3,
        out_specs=vmem,
        scratch_shapes=[
            pltpu.VMEM(w_gate.shape[1:], BF16),
            pltpu.VMEM(w_up.shape[1:], BF16),
            pltpu.VMEM(w_down.shape[1:], BF16),
            pltpu.VMEM((2, EXPERTS * BLOCK, 8 * TOK), BF16),
            pltpu.VMEM((2, 8 * TOK, EXPERTS * BLOCK), BF16),
            pltpu.VMEM((2, EXPERTS, LANES), jnp.int32),
            pltpu.VMEM((2, EXPERTS, LANES), jnp.int32),
            pltpu.VMEM((STACK, SOURCES * BLOCK), BF16),
            pltpu.VMEM((SOURCES * BLOCK, STACK), BF16),
            pltpu.VMEM((2, 4, CHUNKS * TOK, 2 * LANES), BF16),
            pltpu.VMEM((count, 2, BLOCK, LANES), BF16),
            pltpu.VMEM((ZONES, SOURCES, 2, BLOCK, LANES), BF16),
            pltpu.VMEM((2 * GROUP_ROWS, SLICE), BF16),
            pltpu.VMEM((ZONES, 4, 2 * GROUP_ROWS, LANES), BF16),
            pltpu.VMEM((ZONES, 4, 2 * GROUP_ROWS, LANES), BF16),
            pltpu.VMEM((ZONES, 4, 2 * GROUP_ROWS, LANES), F32),
            pltpu.VMEM((ZONES, 4, 2 * GROUP_ROWS, LANES), BF16),
            pltpu.VMEM((ZONES, 3, 2 * GROUP_ROWS, LANES), BF16),
            pltpu.VMEM((ZONES, MEMBERS, 4, GROUP_ROWS, LANES), BF16),
            pltpu.VMEM((2, count, BLOCK, LANES), BF16),
            pltpu.VMEM((2, count, BLOCK, LANES), BF16),
            dma((3,)),
            dma((2,)),
            dma((2,)),
            dma((ZONES,)),
            dma((ZONES,)),
            dma,
            dma((ZONES,)),
            dma((ZONES,)),
            dma((ZONES,)),
            dma((ZONES,)),
            dma((ZONES, 6)),
            dma((ZONES, 6)),
            dma((2,)),
            dma((2,)),
        ],
        compiler_params=pltpu.CompilerParams(
            collective_id=0, has_side_effects=True, vmem_limit_bytes=58 * 2**20
        ),
    )(ids, weight, valid[0], out_grad[0], gate_pre[0], up_pre[0], w_gate[0], w_up[0], w_down[0])
    return out[None]


def solution(mesh):
    placed = (
        P("pipe", None, "expert", None),
        P("pipe", None, "expert", None),
        P("pipe", None, "expert", None),
        P("pipe", None, "expert"),
        P("pipe", None, None, "expert"),
        P("pipe", None, None, "expert"),
        P("pipe", "expert", None),
        P("pipe", "expert", None),
        P("pipe", None, "expert"),
    )
    return jax.shard_map(
        body, mesh=mesh, in_specs=placed, out_specs=P("pipe", None, "expert", None), check_vma=False
    )
```

time: 169 us -> 147 us (0.87)
  Pallas kernels: 162 us -> 144 us
  local copies, waits for them, and re-layouts: 4.96 us -> 2.85 us
    pallas_call x1, Pallas kernels: 162 us -> 144 us  [body(): pl.pallas_call(kernel, out_shape=jax.ShapeDtypeStruct(out_grad.shape[1:],...]
where the time goes in v2:
time: 147 us
  Pallas kernels  144 us (98%)
  local copies, waits for them, and re-layouts  2.85 us (2%)
    pallas_call x1, Pallas kernels, body(): pl.pallas_call(kernel, out_shape=jax.ShapeDtypeStruct(out_grad.shape[1:],...  144 us

profile of v2, /device:TPU:1, one launch (start us, length us, event | category | flops | bytes accessed | tf_op | source)
XLA Modules:
  0.0 147.0 jit_solution(12831960920497671167)
XLA Ops:
  0.0 144.1 %shard_map.91 = bf16[2,64,7168]{2,1,0:T(8,128)(2,1)} custom-call(s32[2,1,64]{2,1,0:T(1,128)} %bitcast.21, f32[2,1,64]{2,1,0:T(1,128)} %bitcast.22, s32[2,64]{1,0:T(2,128)} %bitcast.23, bf16[2,64,7168]{2,1,0:T(8,128)(2,1)} %bitcast.15, bf16[2,576,128]{2,1,0:T(8,128)(2,1)} %bitcast.19, bf16[2,576,128]{2,1,0:T(8,128)(2,1)} %bitcast.20, ...), custom_call_target="tpu_custom_call" | custom-call | tf_op jit(solution)/shard_map/pallas_call | solution.py:505
  144.1 2.8 %copy.13 = bf16[1,2,64,7168]{3,2,1,0:T(8,128)(2,1)} copy(bf16[1,2,64,7168]{3,2,1,0:T(8,128)(2,1)} %bitcast.14) | data formatting | bytes 3670016

commit v3 on v2

--- a/solution.py
+++ b/solution.py
@@ -17,6 +17,7 @@
 GROUP_ROWS = SOURCES * CAP
 STACK = CHUNKS * GROUP_ROWS
 ZONES = 4
+HALVES = (((0, 0), (0, 1)), ((2, 0), (2, 1)), ((1, 0), (3, 0)), ((1, 1), (3, 1)))
 GATE = (0, 3)
 UP = (1, 2)
 MESH = pl.DeviceIdType.MESH
@@ -67,13 +68,16 @@
     ids_ref,
     weight_ref,
     valid_ref,
-    x_ref,
-    gate_ref,
-    up_ref,
+    x_hbm,
+    gate_hbm,
+    up_hbm,
     wg_hbm,
     wu_hbm,
     wd_hbm,
     out_ref,
+    x_ref,
+    gate_ref,
+    up_ref,
     wg_ref,
     wu_ref,
     wd_ref,
@@ -122,6 +126,10 @@
     has_low, has_high = p > 0, p < pipes - 1
     low, high = jnp.maximum(p - 1, 0), jnp.minimum(p + 1, pipes - 1)
 
+    onward = ((has_low, low), (has_high, high))
+
+    tokens = pltpu.make_async_copy(x_hbm, x_ref, w_sem.at[0])
+    tokens.start()
     barrier = pltpu.get_barrier_semaphore()
 
     def greet(i):
@@ -140,9 +148,11 @@
         pl.semaphore_signal(barrier, inc=1, device_id=(high, me), device_id_type=MESH)
 
     weights = [
-        pltpu.make_async_copy(wd_hbm, wd_ref, w_sem.at[0]),
-        pltpu.make_async_copy(wg_hbm, wg_ref, w_sem.at[1]),
-        pltpu.make_async_copy(wu_hbm, wu_ref, w_sem.at[2]),
+        pltpu.make_async_copy(wd_hbm, wd_ref, w_sem.at[1]),
+        pltpu.make_async_copy(wg_hbm, wg_ref, w_sem.at[2]),
+        pltpu.make_async_copy(wu_hbm, wu_ref, w_sem.at[3]),
+        pltpu.make_async_copy(gate_hbm, gate_ref, w_sem.at[4]),
+        pltpu.make_async_copy(up_hbm, up_ref, w_sem.at[5]),
     ]
     for copy in weights:
         copy.start()
@@ -169,6 +179,9 @@
         ids_out[m] = jnp.broadcast_to(
             jnp.concatenate([ids, jnp.zeros_like(ids)], axis=1), (EXPERTS, LANES)
         )
+
+    tokens.wait()
+    for m in range(2):
         same = iota((TOK, TOK), 0) == iota((TOK, TOK), 1)
         scale = weight_ref[m] * valid_ref[m : m + 1].astype(F32)
         scale = jnp.sum(jnp.where(same, scale, 0.0), axis=1, keepdims=True)
@@ -179,8 +192,8 @@
                     x_ref[m, :, col : col + LANES].astype(F32) * scale
                 ).astype(BF16)
 
-    def form(dz):
-        zone = zone_of(dz)
+    def form(k):
+        zone = zone_of(k)
 
         def part(i):
             m, pair = i // 4, lax.rem(i, 4)
@@ -194,18 +207,30 @@
 
         loop(8, part)
 
-    def dispatch(dz):
-        zone, c = zone_of(dz), (ZONES - dz) % ZONES
-        first_other = 1 if dz == 0 else 0
+    def dispatch(c):
+        if c < 2:
+            zone = zone_of(HALVES[c][0][0])
+            skip = 1 if c == 0 else 0
+
+            def go(i):
+                t = lax.rem(spot + skip + i, SOURCES)
+                d = zone * SOURCES + t
+                remote(send_ref.at[d], recv_ref.at[c, spot], d_send.at[c], d_recv.at[c], (p, d)).start()
+
+            loop(SOURCES - skip, go)
+            if c == 0:
+                pltpu.make_async_copy(send_ref.at[me], recv_ref.at[0, spot], d_local).start()
+            return
 
         def go(i):
-            t = lax.rem(spot + first_other + i, SOURCES)
-            d = zone * SOURCES + t
-            remote(send_ref.at[d], recv_ref.at[c, spot], d_send.at[dz], d_recv.at[c], (p, d)).start()
-
-        loop(SOURCES - first_other, go)
-        if dz == 0:
-            pltpu.make_async_copy(send_ref.at[me], recv_ref.at[0, spot], d_local).start()
+            t = lax.rem(spot + i, SOURCES)
+            for h, (back, m) in enumerate(HALVES[c]):
+                d = zone_of(ZONES - back) * SOURCES + t
+                remote(
+                    send_ref.at[d, m], recv_ref.at[c, spot, h], d_send.at[c], d_recv.at[c], (p, d)
+                ).start()
+
+        loop(SOURCES, go)
 
     def hidden(c):
         if c == 0:
@@ -213,7 +238,7 @@
             drain(recv_ref.at[c, 0], d_local)
         else:
             drain(recv_ref.at[c], d_recv.at[c])
-        both = [recv_ref[c, :, m].reshape(SOURCES * BLOCK, LANES) for m in range(2)]
+        both = [recv_ref[c, :, h].reshape(SOURCES * BLOCK, LANES) for h in range(2)]
         rows = dot(pack_ref[...], jnp.concatenate(both, axis=1)).astype(BF16)
         for m in range(2):
             for j in range(CHUNKS):
@@ -269,17 +294,17 @@
 
     def activation(c):
         drain(yin_ref.at[c], s_recv.at[c])
-        saved = pl.ds(pl.multiple_of(zone_of(c) * GROUP_ROWS, 16), GROUP_ROWS)
-        for m in range(2):
-            at = pl.ds(GROUP_ROWS * m, GROUP_ROWS)
+        for h, (back, m) in enumerate(HALVES[c]):
+            at = pl.ds(GROUP_ROWS * h, GROUP_ROWS)
+            saved = pl.ds(pl.multiple_of(zone_of(back) * GROUP_ROWS, 16), GROUP_ROWS)
             o = own_ref[c, y, at, :]
             for k in range(3):
                 o = o + yin_ref[c, k, at, :].astype(F32)
             g = gate_ref[m, saved, :].astype(F32)
             u = up_ref[m, saved, :].astype(F32)
             sig = jax.nn.sigmoid(g)
-            grads_ref[c, member, GATE[m]] = (o * u * sig * (1.0 + g * (1.0 - sig))).astype(BF16)
-            grads_ref[c, member, UP[m]] = (o * g * sig).astype(BF16)
+            grads_ref[c, member, GATE[h]] = (o * u * sig * (1.0 + g * (1.0 - sig))).astype(BF16)
+            grads_ref[c, member, UP[h]] = (o * g * sig).astype(BF16)
         share(c, 0, other, member, 0, 3)
         share(c, 1, right, member, 0, 4)
         share(c, 1, left, member, 0, 4)
@@ -312,7 +337,6 @@
         share(c, 4, two, over_one, 2, 1)
 
     def rows_out(c):
-        zone = zone_of(c)
         drain(grads_ref.at[c, 0, pl.ds(0, 3)], g_recv.at[c, 4])
         drain(grads_ref.at[c, pl.ds(0, 4), 0], g_recv.at[c, 5])
 
@@ -339,17 +363,20 @@
             axis=0,
         )
         r = dot(unpack_ref[...], r).astype(BF16)
-        for m, wanted, target in ((0, has_low, low), (1, has_high, high)):
-            ret_ref[m, pl.ds(zone * SOURCES, SOURCES)] = r[:, LANES * m : LANES * (m + 1)].reshape(
-                SOURCES, BLOCK, LANES
-            )
-
-            @pl.when(wanted)
+        for h, (back, m) in enumerate(HALVES[c]):
+            ret_ref[c, h] = r[:, LANES * h : LANES * (h + 1)].reshape(SOURCES, BLOCK, LANES)
+            zone = zone_of(back)
+
+            @pl.when(onward[m][0])
             def _():
-                def go(k):
-                    q = zone * SOURCES + lax.rem(me + k, SOURCES)
+                def go(i):
+                    t = lax.rem(spot + i, SOURCES)
                     remote(
-                        ret_ref.at[m, q], home_ref.at[m, me], r_send.at[m], r_recv.at[m], (target, q)
+                        ret_ref.at[c, h, t],
+                        home_ref.at[m, me],
+                        r_send.at[m],
+                        r_recv.at[m],
+                        (onward[m][1], zone * SOURCES + t),
                     ).start()
 
                 loop(SOURCES, go)
@@ -421,11 +448,13 @@
     pl.semaphore_wait(
         barrier, count - 1 + jnp.where(has_low, 1, 0) + jnp.where(has_high, 1, 0)
     )
-    dispatch(2)
+    dispatch(1)
     form(0)
     dispatch(0)
+    form(1)
     form(3)
-    form(1)
+    dispatch(2)
+    dispatch(3)
 
     to_low = remote(ids_out.at[0], ids_in.at[0], ids_send.at[0], ids_recv.at[0], (low, me))
     to_high = remote(ids_out.at[1], ids_in.at[1], ids_send.at[1], ids_recv.at[1], (high, me))
@@ -440,36 +469,36 @@
 
     build_pack()
     weights[0].wait()
+    weights[3].wait()
+    weights[4].wait()
     hidden(0)
     reduce_x(0)
-    dispatch(3)
     activation(0)
+    hidden(1)
+    pass_on(0)
+    reduce_x(1)
     hidden(2)
-    pass_on(0)
-    dispatch(1)
-    hidden(1)
+    pass_far(0)
+    activation(1)
+    build_unpack()
     reduce_x(2)
+    pass_on(1)
+    hidden(3)
     activation(2)
-    hidden(3)
-    reduce_x(1)
-    pass_on(2)
-    pass_far(2)
-    reduce_x(3)
-    build_unpack()
+    pass_far(1)
     weights[1].wait()
     weights[2].wait()
-    activation(1)
+    reduce_x(3)
+    pass_on(2)
+    rows_out(1)
+    activation(3)
+    pass_far(2)
+    selections()
+    pass_on(3)
     rows_out(2)
-    pass_on(1)
-    pass_far(0)
-    selections()
-    activation(3)
-    pass_far(1)
-    pass_on(3)
-    rows_out(1)
     pass_far(3)
+    rows_out(0)
     rows_out(3)
-    rows_out(0)
     finish(0, has_high)
     finish(1, has_low)
 
@@ -505,9 +534,12 @@
     out = pl.pallas_call(
         kernel,
         out_shape=jax.ShapeDtypeStruct(out_grad.shape[1:], BF16),
-        in_specs=[vmem] * 6 + [hbm] * 3,
+        in_specs=[vmem] * 3 + [hbm] * 6,
         out_specs=vmem,
         scratch_shapes=[
+            pltpu.VMEM(out_grad.shape[1:], BF16),
+            pltpu.VMEM(gate_pre.shape[1:], BF16),
+            pltpu.VMEM(up_pre.shape[1:], BF16),
             pltpu.VMEM(w_gate.shape[1:], BF16),
             pltpu.VMEM(w_up.shape[1:], BF16),
             pltpu.VMEM(w_down.shape[1:], BF16),
@@ -527,9 +559,9 @@
             pltpu.VMEM((ZONES, 4, 2 * GROUP_ROWS, LANES), BF16),
             pltpu.VMEM((ZONES, 3, 2 * GROUP_ROWS, LANES), BF16),
             pltpu.VMEM((ZONES, MEMBERS, 4, GROUP_ROWS, LANES), BF16),
+            pltpu.VMEM((ZONES, 2, SOURCES, BLOCK, LANES), BF16),
             pltpu.VMEM((2, count, BLOCK, LANES), BF16),
-            pltpu.VMEM((2, count, BLOCK, LANES), BF16),
-            dma((3,)),
+            dma((6,)),
             dma((2,)),
             dma((2,)),
             dma((ZONES,)),

time: 147 us -> 135 us (0.918)
  Pallas kernels: 144 us -> 132 us
    pallas_call x1, Pallas kernels: 144 us -> 132 us  [body(): pl.pallas_call(kernel, out_shape=jax.ShapeDtypeStruct(out_grad.shape[1:],...]
where the time goes in v3:
time: 135 us
  Pallas kernels  132 us (98%)
  local copies, waits for them, and re-layouts  2.85 us (2%)
    pallas_call x1, Pallas kernels, body(): pl.pallas_call(kernel, out_shape=jax.ShapeDtypeStruct(out_grad.shape[1:],...  132 us
    unnamed x1, local copies, waits for them, and re-layouts  2.85 us

profile of v3, /device:TPU:1, one launch (start us, length us, event | category | flops | bytes accessed | tf_op | source)
XLA Modules:
  0.0 135.0 jit_solution(88529376010866945)
XLA Ops:
  0.0 132.2 %shard_map.91 = bf16[2,64,7168]{2,1,0:T(8,128)(2,1)} custom-call(s32[2,1,64]{2,1,0:T(1,128)} %bitcast.21, f32[2,1,64]{2,1,0:T(1,128)} %bitcast.22, s32[2,64]{1,0:T(2,128)} %bitcast.23, bf16[2,64,7168]{2,1,0:T(8,128)(2,1)} %bitcast.15, bf16[2,576,128]{2,1,0:T(8,128)(2,1)} %bitcast.19, bf16[2,576,128]{2,1,0:T(8,128)(2,1)} %bitcast.20, ...), custom_call_target="tpu_custom_call" | custom-call | tf_op jit(solution)/shard_map/pallas_call | solution.py:534
  132.2 2.8 %copy.13 = bf16[1,2,64,7168]{3,2,1,0:T(8,128)(2,1)} copy(bf16[1,2,64,7168]{3,2,1,0:T(8,128)(2,1)} %bitcast.14) | data formatting | bytes 3670016

commit v4 on v3

--- a/solution.py
+++ b/solution.py
@@ -87,7 +87,7 @@
     ids_in,
     pack_ref,
     unpack_ref,
-    scaled_ref,
+    scale_ref,
     send_ref,
     recv_ref,
     rows_ref,
@@ -175,22 +175,15 @@
 
     for m in range(2):
         ids = ids_ref[m]
-        sel_ref[m] = selection(ids).astype(BF16)
+        sel = selection(ids)
+        sel_ref[m] = sel.astype(BF16)
         ids_out[m] = jnp.broadcast_to(
             jnp.concatenate([ids, jnp.zeros_like(ids)], axis=1), (EXPERTS, LANES)
         )
-
+        scale = weight_ref[m] * valid_ref[m : m + 1].astype(F32)
+        scale = jnp.concatenate([scale] * 8, axis=1)
+        scale_ref[m] = jnp.sum(sel * scale, axis=1, keepdims=True)
     tokens.wait()
-    for m in range(2):
-        same = iota((TOK, TOK), 0) == iota((TOK, TOK), 1)
-        scale = weight_ref[m] * valid_ref[m : m + 1].astype(F32)
-        scale = jnp.sum(jnp.where(same, scale, 0.0), axis=1, keepdims=True)
-        for j in range(CHUNKS):
-            for s in range(MEMBERS):
-                col = s * SLICE + j * LANES
-                scaled_ref[m, s // 2, TOK * j : TOK * (j + 1), LANES * (s % 2) : LANES * (s % 2 + 1)] = (
-                    x_ref[m, :, col : col + LANES].astype(F32) * scale
-                ).astype(BF16)
 
     def form(k):
         zone = zone_of(k)
@@ -198,7 +191,18 @@
         def part(i):
             m, pair = i // 4, lax.rem(i, 4)
             rows = pl.ds(pl.multiple_of(zone * 2 * BLOCK, 2 * BLOCK), 2 * BLOCK)
-            o = dot(sel_ref[m, rows, 0 : CHUNKS * TOK], scaled_ref[m, pair]).astype(BF16)
+            x = [
+                jnp.concatenate(
+                    [
+                        x_ref[m, :, pl.ds(pl.multiple_of((2 * pair + k) * SLICE, LANES) + LANES * j, LANES)]
+                        for k in range(2)
+                    ],
+                    axis=1,
+                )
+                for j in range(CHUNKS)
+            ]
+            o = dot(sel_ref[m, rows, 0 : CHUNKS * TOK], jnp.concatenate(x, axis=0))
+            o = (o * scale_ref[m, rows, :]).astype(BF16)
             for e in range(2):
                 for k in range(2):
                     send_ref[zone * SOURCES + e * MEMBERS + 2 * pair + k, m] = o[
@@ -476,14 +480,14 @@
     activation(0)
     hidden(1)
     pass_on(0)
+    hidden(2)
     reduce_x(1)
-    hidden(2)
     pass_far(0)
     activation(1)
     build_unpack()
+    hidden(3)
     reduce_x(2)
     pass_on(1)
-    hidden(3)
     activation(2)
     pass_far(1)
     weights[1].wait()
@@ -493,8 +497,8 @@
     rows_out(1)
     activation(3)
     pass_far(2)
+    pass_on(3)
     selections()
-    pass_on(3)
     rows_out(2)
     pass_far(3)
     rows_out(0)
@@ -549,7 +553,7 @@
             pltpu.VMEM((2, EXPERTS, LANES), jnp.int32),
             pltpu.VMEM((STACK, SOURCES * BLOCK), BF16),
             pltpu.VMEM((SOURCES * BLOCK, STACK), BF16),
-            pltpu.VMEM((2, 4, CHUNKS * TOK, 2 * LANES), BF16),
+            pltpu.VMEM((2, EXPERTS * BLOCK, 1), F32),
             pltpu.VMEM((count, 2, BLOCK, LANES), BF16),
             pltpu.VMEM((ZONES, SOURCES, 2, BLOCK, LANES), BF16),
             pltpu.VMEM((2 * GROUP_ROWS, SLICE), BF16),

time: 135 us -> 132 us (0.978)
  Pallas kernels: 132 us -> 129 us
    pallas_call x1, Pallas kernels: 132 us -> 129 us  [body(): pl.pallas_call(kernel, out_shape=jax.ShapeDtypeStruct(out_grad.shape[1:],...]
where the time goes in v4:
time: 132 us
  Pallas kernels  129 us (98%)
  local copies, waits for them, and re-layouts  2.85 us (2%)
    pallas_call x1, Pallas kernels, body(): pl.pallas_call(kernel, out_shape=jax.ShapeDtypeStruct(out_grad.shape[1:],...  129 us
    unnamed x1, local copies, waits for them, and re-layouts  2.85 us

profile of v4, /device:TPU:1, one launch (start us, length us, event | category | flops | bytes accessed | tf_op | source)
XLA Modules:
  0.0 132.0 jit_solution(5576761489299278595)
XLA Ops:
  0.0 129.2 %shard_map.91 = bf16[2,64,7168]{2,1,0:T(8,128)(2,1)} custom-call(s32[2,1,64]{2,1,0:T(1,128)} %bitcast.21, f32[2,1,64]{2,1,0:T(1,128)} %bitcast.22, s32[2,64]{1,0:T(2,128)} %bitcast.23, bf16[2,64,7168]{2,1,0:T(8,128)(2,1)} %bitcast.15, bf16[2,576,128]{2,1,0:T(8,128)(2,1)} %bitcast.19, bf16[2,576,128]{2,1,0:T(8,128)(2,1)} %bitcast.20, ...), custom_call_target="tpu_custom_call" | custom-call | tf_op jit(solution)/shard_map/pallas_call | solution.py:538
  129.2 2.8 %copy.13 = bf16[1,2,64,7168]{3,2,1,0:T(8,128)(2,1)} copy(bf16[1,2,64,7168]{3,2,1,0:T(8,128)(2,1)} %bitcast.14) | data formatting | bytes 3670016

commit v5 on v4

--- a/solution.py
+++ b/solution.py
@@ -344,31 +344,13 @@
         drain(grads_ref.at[c, 0, pl.ds(0, 3)], g_recv.at[c, 4])
         drain(grads_ref.at[c, pl.ds(0, 4), 0], g_recv.at[c, 5])
 
-        def whole(quarters):
-            rows = [
-                jnp.concatenate([grads_ref[c, k, q] for k in range(MEMBERS)], axis=1)
-                for q in quarters
-            ]
-            return jnp.concatenate(rows, axis=0)
-
-        gate, up = whole(GATE), whole(UP)
-        r = (dot_t(gate, wg_ref[...]) + dot_t(up, wu_ref[...])).astype(BF16)
-        r = jnp.concatenate(
-            [
-                jnp.concatenate(
-                    [
-                        r[GROUP_ROWS * m : GROUP_ROWS * (m + 1), LANES * j : LANES * (j + 1)]
-                        for m in range(2)
-                    ],
-                    axis=1,
-                )
-                for j in range(CHUNKS)
-            ],
-            axis=0,
-        )
-        r = dot(unpack_ref[...], r).astype(BF16)
         for h, (back, m) in enumerate(HALVES[c]):
-            ret_ref[c, h] = r[:, LANES * h : LANES * (h + 1)].reshape(SOURCES, BLOCK, LANES)
+            gate = jnp.concatenate([grads_ref[c, k, GATE[h]] for k in range(MEMBERS)], axis=1)
+            up = jnp.concatenate([grads_ref[c, k, UP[h]] for k in range(MEMBERS)], axis=1)
+            r = (dot_t(gate, wg_ref[...]) + dot_t(up, wu_ref[...])).astype(BF16)
+            r = jnp.concatenate([r[:, LANES * j : LANES * (j + 1)] for j in range(CHUNKS)], axis=0)
+            r = dot(unpack_ref[...], r).astype(BF16)
+            ret_ref[c, h] = r.reshape(SOURCES, BLOCK, LANES)
             zone = zone_of(back)
 
             @pl.when(onward[m][0])

time: 132 us -> 135 us (1.023)
  Pallas kernels: 129 us -> 132 us
    pallas_call x1, Pallas kernels: 129 us -> 132 us  [body(): pl.pallas_call(kernel, out_shape=jax.ShapeDtypeStruct(out_grad.shape[1:],...]
where the time goes in v5:
time: 135 us; the launch traced here: 134 us
  Pallas kernels  132 us (98%)
  local copies, waits for them, and re-layouts  2.85 us (2%)
    pallas_call x1, Pallas kernels, body(): pl.pallas_call(kernel, out_shape=jax.ShapeDtypeStruct(out_grad.shape[1:],...  132 us
    unnamed x1, local copies, waits for them, and re-layouts  2.85 us

profile of v5, /device:TPU:1, one launch (start us, length us, event | category | flops | bytes accessed | tf_op | source)
XLA Modules:
  0.0 134.4 jit_solution(9945640336912945196)
XLA Ops:
  0.0 131.5 %shard_map.91 = bf16[2,64,7168]{2,1,0:T(8,128)(2,1)} custom-call(s32[2,1,64]{2,1,0:T(1,128)} %bitcast.21, f32[2,1,64]{2,1,0:T(1,128)} %bitcast.22, s32[2,64]{1,0:T(2,128)} %bitcast.23, bf16[2,64,7168]{2,1,0:T(8,128)(2,1)} %bitcast.15, bf16[2,576,128]{2,1,0:T(8,128)(2,1)} %bitcast.19, bf16[2,576,128]{2,1,0:T(8,128)(2,1)} %bitcast.20, ...), custom_call_target="tpu_custom_call" | custom-call | tf_op jit(solution)/shard_map/pallas_call | solution.py:520
  131.5 2.8 %copy.13 = bf16[1,2,64,7168]{3,2,1,0:T(8,128)(2,1)} copy(bf16[1,2,64,7168]{3,2,1,0:T(8,128)(2,1)} %bitcast.14) | data formatting | bytes 3670016
